TPU v7x, 32 devices: a whole 2x2x4 slice. The times are simulated.
32 devices in a mesh: grp: 2 (over x), view: 4 (over y, core), slab: 4 (over z).
Axes of the slice: x: 2, y: 2, z: 4, core: 2. Of those that a mesh axis runs over, the one named last changes fastest.
Arguments:
- volume: float32 [16, 512, 512], P(('grp', 'slab'), 'view'), parts along dimension 0, may hold values from 0 to 2
- measured: float32 [8, 1024, 128], P(('grp', 'view')), parts along dimension 0, may hold values from -6 to 6
- weights: float32 [8, 1024, 128], P(('grp', 'view')), parts along dimension 0, may hold values from 0.25 to 4
- templates: bfloat16 [8, 64, 128], replicated, may hold values from -0.078125 to 0.078125
- pixel_rows: int32 [4, 65536], P('view', 'slab'), may hold values from 0 to 1023, as said below
- voxel_cols: int32 [4, 65536], P('view', 'slab'), may hold values from 0 to 32767, as said below
- template_ids: int32 [4, 65536], P('view', 'slab'), may hold values from 0 to 7
- curvature: float32 [16, 512, 512], P(('grp', 'slab'), 'view'), parts along dimension 0, may hold values from 1 to 4
Outputs:
- updated: float32 [16, 512, 512], P(('grp', 'slab'), 'view'), parts along dimension 0
There are 2 independent parts, one for each index of `grp`. A program takes and returns all parts, laid end to end along the dimension named above; an argument that names none is the same for every part. Nothing has to cross between parts.
Inputs may be any that keep to these rules, and one draw needn't show every extreme that they name: `voxel_cols`: A view's list is made of groups of 512 consecutive entries; entry k lies in group q = k // 512 and names a voxel block of z-slab k // 16384, one of the blocks q * 256 to (q + 1) * 256 - 1; in every group the first 256 entries name each of these blocks once. `pixel_rows`: entry k, in group q = k // 512 and with w = (q % 32) % 8, names a pixel block of w * 128 to (w + 1) * 128 - 1; in every group the first 128 entries name each of these once.
All inputs are finite; a program needn't handle non-finite values.
Results may differ from a plain program's by a relative error of at most 0.0023.
Values may be sent and summed in bfloat16 or wider, within the bound.
A program may use at most 192 MiB of HBM per device.

v0:
```python
import functools

import jax
import jax.numpy as jnp
from jax import lax
from jax.experimental import pallas as pl
from jax.experimental.pallas import tpu as pltpu
from jax.sharding import PartitionSpec as P

prior_weight = 0.25
MESH = pl.DeviceIdType.MESH
f32 = jnp.float32
bf16 = jnp.bfloat16
NT = (((1,), (1,)), ((), ()))


def slope(gap):
    power = jnp.exp(0.8 * jnp.log(jnp.maximum(jnp.abs(gap), 1e-37)))
    inverse = 1.0 / (1.0 + power)
    return gap * inverse * (2.0 - 0.8 * power * inverse)


def two_terms(value):
    high = value.astype(bf16)
    return high, (value - high.astype(f32)).astype(bf16)


def kernel(
    dims,
    vol_ref, meas_ref, wt_ref, t_ref, row_ref, col_ref, kind_ref, curv_ref,
    out_ref,
    vol_t, part, r_recv, l_recv, r_send, l_send, resid_t, back, sib_in, y_in,
    z_send, z_lo, z_hi, y_lo, y_hi, prior,
    gs_sib, gs_y, gs_relay, g_recv, hz_s, hz_r, hy_s, hy_r,
    rs_s, rs_r, ls_s, ls_r, bs_s, bs_r, by_s, by_r,
):
    vc, sc, z_local, y_own, chunk_rows, kinds, vw, windows, ypg, group = dims
    ny = y_own // chunk_rows
    nych = vc // 2
    me = lax.axis_index("view")
    slab = lax.axis_index("slab")
    y = me // 2
    c = me % 2
    sib = y * 2 + 1 - c

    def remote(src, dst, ss, rs, **where):
        return pltpu.make_async_remote_copy(
            src_ref=src, dst_ref=dst, send_sem=ss, recv_sem=rs,
            device_id=where, device_id_type=MESH,
        )

    barrier = pltpu.get_barrier_semaphore()

    def greet(**where):
        pl.semaphore_signal(barrier, inc=1, device_id=where, device_id_type=MESH)

    for ref in (r_recv, l_recv, z_lo, z_hi, y_lo, y_hi):
        ref[...] = jnp.zeros_like(ref)
    greet(view=sib)
    for dy in range(1, nych):
        greet(view=lax.rem(y + dy, nych) * 2 + c)
    has_left, has_right = slab > 0, slab < sc - 1
    has_low, has_high = me > 0, me < vc - 1
    pl.when(has_left)(lambda: greet(slab=slab - 1))
    pl.when(has_right)(lambda: greet(slab=slab + 1))
    pl.when(has_low)(lambda: greet(view=me - 1))
    pl.when(has_high)(lambda: greet(view=me + 1))

    for z in range(z_local):
        for ch in range(ny):
            rows = vol_ref[z, pl.ds(ch * chunk_rows, chunk_rows), :]
            tall = jnp.concatenate([rows[:, k * 128:(k + 1) * 128] for k in range(4)], axis=0)
            turned = tall.T
            vol_t[me, z * ny + ch] = jnp.concatenate(
                [turned[:vw], turned[vw:]], axis=1
            ).astype(bf16)
    z_send[0] = vol_ref[0].astype(bf16)
    z_send[1] = vol_ref[z_local - 1].astype(bf16)

    pl.semaphore_wait(
        barrier,
        nych + jnp.where(has_left, 1, 0) + jnp.where(has_right, 1, 0)
        + jnp.where(has_low, 1, 0) + jnp.where(has_high, 1, 0),
    )

    def gather_y(dy):
        other = lax.rem(y + dy, nych)
        return remote(vol_t.at[me], vol_t.at[me], gs_y.at[dy], g_recv.at[me], view=other * 2 + c)

    gather_sib = remote(vol_t.at[me], vol_t.at[me], gs_sib, g_recv.at[me], view=sib)
    for dy in range(1, nych):
        gather_y(dy).start()
    gather_sib.start()

    z_down = remote(z_send.at[0], z_hi, hz_s.at[0], hz_r.at[0], slab=slab - 1)
    z_up = remote(z_send.at[1], z_lo, hz_s.at[1], hz_r.at[1], slab=slab + 1)
    y_down = remote(vol_ref.at[:, 0:8], y_hi, hy_s.at[0], hy_r.at[0], view=me - 1)
    y_up = remote(vol_ref.at[:, y_own - 8:y_own], y_lo, hy_s.at[1], hy_r.at[1], view=me + 1)
    pl.when(has_left)(z_down.start)
    pl.when(has_right)(z_up.start)
    pl.when(has_low)(y_down.start)
    pl.when(has_high)(y_up.start)

    vox_count = chunk_rows * 8
    pix = meas_ref.shape[1] // windows
    vox_iota = lax.broadcasted_iota(jnp.int32, (vox_count, group), 0)
    pix_iota = lax.broadcasted_iota(jnp.int32, (pix, group), 0)

    def entries(q):
        here = pl.ds(pl.multiple_of(q * group, group), group)
        col = col_ref[:, here] & (vox_count - 1)
        spot = (col & 1) * (vox_count // 2) + ((col >> 1) & 3) * chunk_rows + (col >> 3)
        return row_ref[:, here] & (pix - 1), spot, kind_ref[:, here]

    def one_hot(iota, spot):
        return jnp.where(iota == spot, 1.0, 0.0).astype(bf16)

    def relay(o):
        return remote(vol_t.at[o], vol_t.at[o], gs_relay.at[o // 2], g_recv.at[o], view=sib)

    def forward(w, k):
        yc = w + windows * k
        owner = yc // ny
        ch = yc % ny

        @pl.when((ch == 0) & (owner != me))
        def _():
            relay(owner).wait_recv()

        @pl.when((ch == 0) & (owner % 2 == c) & (owner // 2 != y))
        def _():
            relay(owner).start()

        total = None
        for z in range(z_local):
            rows, spots, kind = entries(z * ypg + yc)
            picked = jnp.dot(
                vol_t[owner, z * ny + ch], one_hot(vox_iota, spots), preferred_element_type=f32
            )
            spread = jnp.concatenate(
                [jnp.where(kind == t, picked, 0.0).astype(bf16) for t in range(kinds)], axis=0
            )
            added = lax.dot_general(
                one_hot(pix_iota, rows), spread, NT, preferred_element_type=f32
            )
            total = added if total is None else total + added
        high, rest = two_terms(total)
        return jnp.dot(high, t_ref[...], preferred_element_type=f32) + jnp.dot(
            rest, t_ref[...], preferred_element_type=f32
        )

    nk = ypg // windows
    k_base = (2 * y * ny) // windows

    def order(i):
        return lax.rem(i + c * ny, windows)

    for p in range(nk - 1):
        def pass_step(i, carry, p=p):
            w = order(i)
            value = forward(w, lax.rem(k_base + p, nk))
            if p == 0:
                part[w] = value
            else:
                part[w] = part[w] + value
            return carry
        lax.fori_loop(0, windows, pass_step, 0)

    def right_copy(i):
        return remote(r_send.at[i], r_recv.at[i], rs_s.at[i], rs_r.at[i], slab=slab + 1)

    def left_copy(i):
        return remote(l_send.at[i], l_recv.at[i], ls_s.at[i], ls_r.at[i], slab=slab - 1)

    def streams(i):
        ri = i - slab
        li = i - (sc - 1 - slab)

        @pl.when((ri >= 0) & (ri < windows))
        def _():
            pl.when(has_left)(lambda: right_copy(ri).wait_recv())

            @pl.when(has_right)
            def _():
                r_send[ri] = part[order(ri)] + r_recv[ri]
                right_copy(ri).start()

        @pl.when((li >= 0) & (li < windows))
        def _():
            pl.when(has_right)(lambda: left_copy(li).wait_recv())

            @pl.when(has_left)
            def _():
                l_send[li] = part[order(li)] + l_recv[li]
                left_copy(li).start()

    def last_step(i, carry):
        w = order(i)
        value = forward(w, lax.rem(k_base + nk - 1, nk))
        if nk > 1:
            value = part[w] + value
        part[w] = value
        streams(i)
        return carry

    lax.fori_loop(0, windows, last_step, 0)

    def tail_step(i, carry):
        streams(i)
        return carry

    lax.fori_loop(windows, windows + sc - 1, tail_step, 0)

    def resid_step(i, carry):
        w = order(i)
        here = pl.ds(pl.multiple_of(w * pix, pix), pix)
        proj = part[w] + r_recv[i] + l_recv[i]
        resid = (wt_ref[0, here, :] * (meas_ref[0, here, :] - proj)).astype(bf16)
        turned = lax.dot_general(t_ref[...], resid, NT, preferred_element_type=f32)
        resid_t[w] = jnp.concatenate(two_terms(turned), axis=1)
        return carry

    lax.fori_loop(0, windows, resid_step, 0)

    def backward(owner):
        def step(ch, carry):
            yc = owner * ny + ch
            w = lax.rem(yc, windows)
            for z in range(z_local):
                rows, spots, kind = entries(z * ypg + yc)
                chosen = one_hot(pix_iota, rows)
                wide = jnp.dot(
                    resid_t[w], jnp.concatenate([chosen, chosen], axis=0),
                    preferred_element_type=f32,
                )
                picked = wide[:vw]
                for t in range(1, kinds):
                    picked = jnp.where(kind == t, wide[t * vw:(t + 1) * vw], picked)
                added = lax.dot_general(
                    jnp.concatenate(two_terms(picked), axis=0), one_hot(vox_iota, spots), NT,
                    preferred_element_type=f32,
                )
                back[owner, z * ny + ch] = (added[:vw] + added[vw:]).astype(bf16)
            return carry
        lax.fori_loop(0, ny, step, 0)

    def to_sib(yy):
        return remote(
            back.at[yy * 2 + 1 - c], sib_in.at[yy], bs_s.at[yy], bs_r.at[yy], view=sib
        )

    def to_y(yy):
        return remote(back.at[yy * 2 + c], y_in.at[y], by_s.at[yy], by_r.at[y], view=yy * 2 + c)

    def from_y(yy):
        return remote(back.at[yy * 2 + c], y_in.at[yy], by_s.at[yy], by_r.at[yy], view=yy * 2 + c)

    def far(dy, carry):
        yy = lax.rem(y + dy, nych)
        backward(yy * 2 + 1 - c)
        to_sib(yy).start()
        backward(yy * 2 + c)
        to_sib(yy).wait_recv()
        mine = yy * 2 + c
        back[mine] = (back[mine].astype(f32) + sib_in[yy].astype(f32)).astype(bf16)
        to_y(yy).start()
        return carry

    lax.fori_loop(1, nych, far, 0)
    backward(y * 2 + 1 - c)
    to_sib(y).start()
    backward(me)

    pl.when(has_right)(z_down.wait_recv)
    pl.when(has_left)(z_up.wait_recv)
    pl.when(has_high)(y_down.wait_recv)
    pl.when(has_low)(y_up.wait_recv)
    x_width = vol_ref.shape[2]
    lane = lax.broadcasted_iota(jnp.int32, (y_own, x_width), 1)
    line = lax.broadcasted_iota(jnp.int32, (y_own, x_width), 0)
    one = lambda flag: jnp.where(flag, 1.0, 0.0)
    below = None
    for z in range(z_local):
        v = vol_ref[z]
        gx = jnp.where(lane < x_width - 1, slope(v - pltpu.roll(v, x_width - 1, 1)), 0.0)
        pull = gx - pltpu.roll(gx, 1, 1)
        top = y_hi[z, 0:1, :]
        nxt = jnp.where(line == y_own - 1, top, pltpu.roll(v, y_own - 1, 0))
        gy = slope(v - nxt) * jnp.where(line == y_own - 1, one(has_high), 1.0)
        first = slope(y_lo[z, 7:8, :] - v[0:1, :]) * one(has_low)
        pull = pull + gy - jnp.where(line == 0, first, pltpu.roll(gy, 1, 0))
        if z == 0:
            below = slope(z_lo[...].astype(f32) - v) * one(has_left)
        if z < z_local - 1:
            above = slope(v - vol_ref[z + 1])
        else:
            above = slope(v - z_hi[...].astype(f32)) * one(has_right)
        prior[z] = pull + above - below
        below = above

    to_sib(y).wait_recv()

    def wait_far(dy, carry):
        from_y(lax.rem(y + dy, nych)).wait_recv()
        return carry

    lax.fori_loop(1, nych, wait_far, 0)

    for z in range(z_local):
        for ch in range(ny):
            at = z * ny + ch
            total = back[me, at].astype(f32) + sib_in[y, at].astype(f32)
            for dy in range(1, nych):
                total = total + y_in[lax.rem(y + dy, nych), at].astype(f32)
            half = vox_count // 2
            tall = jnp.concatenate([total[:, :half], total[:, half:]], axis=0).T
            bp = jnp.concatenate(
                [tall[k * chunk_rows:(k + 1) * chunk_rows] for k in range(4)], axis=1
            )
            here = pl.ds(ch * chunk_rows, chunk_rows)
            out_ref[z, here, :] = vol_ref[z, here, :] + (
                bp - prior_weight * prior[z, here, :]
            ) / curv_ref[z, here, :]

    gather_sib.wait_send()
    for dy in range(1, nych):
        gather_y(dy).wait_send()
    pl.when(has_left)(z_down.wait_send)
    pl.when(has_right)(z_up.wait_send)
    pl.when(has_low)(y_down.wait_send)
    pl.when(has_high)(y_up.wait_send)

    def drain_y(dy, carry):
        yy = lax.rem(y + dy, nych)
        relay(yy * 2 + c).wait_send()
        to_sib(yy).wait_send()
        to_y(yy).wait_send()
        return carry

    lax.fori_loop(1, nych, drain_y, 0)
    to_sib(y).wait_send()

    def drain_z(i, carry):
        pl.when(has_right)(lambda: right_copy(i).wait_send())
        pl.when(has_left)(lambda: left_copy(i).wait_send())
        return carry

    lax.fori_loop(0, windows, drain_z, 0)


def per_device(vc, sc, volume, measured, weights, templates, rows, cols, kind_ids, curvature):
    z_local, y_own, x_width = volume.shape
    kinds, vw, pix_width = templates.shape
    group = 512
    chunk_rows = 256 // (x_width // vw)
    windows = measured.shape[1] // 128
    ypg = y_own * vc // chunk_rows
    ny = y_own // chunk_rows
    nych = vc // 2
    tile = (z_local * ny, vw, 256)
    dims = (vc, sc, z_local, y_own, chunk_rows, kinds, vw, windows, ypg, group)
    window = (windows, 128, pix_width)
    dma = pltpu.SemaphoreType.DMA
    vmem = pl.BlockSpec(memory_space=pltpu.VMEM)
    return pl.pallas_call(
        functools.partial(kernel, dims),
        out_shape=jax.ShapeDtypeStruct(volume.shape, f32),
        in_specs=[vmem] * 8,
        out_specs=vmem,
        scratch_shapes=[
            pltpu.VMEM((vc,) + tile, bf16),
            pltpu.VMEM(window, f32),
            pltpu.VMEM(window, f32),
            pltpu.VMEM(window, f32),
            pltpu.VMEM(window, f32),
            pltpu.VMEM(window, f32),
            pltpu.VMEM((windows, kinds * vw, 256), bf16),
            pltpu.VMEM((vc,) + tile, bf16),
            pltpu.VMEM((nych,) + tile, bf16),
            pltpu.VMEM((nych,) + tile, bf16),
            pltpu.VMEM((2, y_own, x_width), bf16),
            pltpu.VMEM((y_own, x_width), bf16),
            pltpu.VMEM((y_own, x_width), bf16),
            pltpu.VMEM((z_local, 8, x_width), f32),
            pltpu.VMEM((z_local, 8, x_width), f32),
            pltpu.VMEM(volume.shape, f32),
            dma, dma((nych,)), dma((nych,)), dma((vc,)),
            dma((2,)), dma((2,)), dma((2,)), dma((2,)),
            dma((windows,)), dma((windows,)), dma((windows,)), dma((windows,)),
            dma((nych,)), dma((nych,)), dma((nych,)), dma((nych,)),
        ],
        compiler_params=pltpu.CompilerParams(
            collective_id=0, has_side_effects=True, vmem_limit_bytes=40 * 1024 * 1024
        ),
    )(
        volume, measured, weights, templates.reshape(kinds * vw, pix_width),
        rows, cols, kind_ids, curvature,
    )


def solution(mesh):
    in_specs = (
        P(("grp", "slab"), "view", None),
        P(("grp", "view"), None, None),
        P(("grp", "view"), None, None),
        P(),
        P("view", "slab"),
        P("view", "slab"),
        P("view", "slab"),
        P(("grp", "slab"), "view", None),
    )
    out_specs = P(("grp", "slab"), "view", None)
    return jax.shard_map(
        functools.partial(per_device, mesh.shape["view"], mesh.shape["slab"]),
        mesh=mesh, in_specs=in_specs, out_specs=out_specs, check_vma=False,
    )
```

profile of v0, /device:TPU:0, one launch (start us, length us, event | category | flops | bytes accessed | tf_op | source)
XLA Modules:
  0.0 69.7 jit_solution(6505290440156322468)
XLA Ops:
  0.0 0.0 copy-start
  0.0 1.0 %copy-done = f32[2,128,512]{2,1,0:T(8,128)S(1)} copy-done((f32[2,128,512]{2,1,0:T(8,128)S(1)}, f32[2,128,512]{2,1,0:T(8,128)}, u32[]{:S(2)}) %copy-start) | copy-done | bytes 524312
  1.0 0.0 copy-start.1
  1.0 1.0 %copy-done.1 = f32[1,1024,128]{2,1,0:T(8,128)S(1)} copy-done((f32[1,1024,128]{2,1,0:T(8,128)S(1)}, f32[1,1024,128]{2,1,0:T(8,128)}, u32[]{:S(2)}) %copy-start.1) | copy-done | bytes 524312
  2.1 0.0 copy-start.2
  2.1 1.0 %copy-done.2 = f32[1,1024,128]{2,1,0:T(8,128)S(1)} copy-done((f32[1,1024,128]{2,1,0:T(8,128)S(1)}, f32[1,1024,128]{2,1,0:T(8,128)}, u32[]{:S(2)}) %copy-start.2) | copy-done | bytes 524312
  3.1 0.0 copy-start.3
  3.1 1.0 %copy-done.3 = f32[2,128,512]{2,1,0:T(8,128)S(1)} copy-done((f32[2,128,512]{2,1,0:T(8,128)S(1)}, f32[2,128,512]{2,1,0:T(8,128)}, u32[]{:S(2)}) %copy-start.3) | copy-done | bytes 524312
  4.2 0.0 copy-start.4
  4.2 0.9 %copy-done.4 = bf16[8,64,128]{2,1,0:T(8,128)(2,1)S(1)} copy-done((bf16[8,64,128]{2,1,0:T(8,128)(2,1)S(1)}, bf16[8,64,128]{2,1,0:T(8,128)(2,1)}, u32[]{:S(2)}) %copy-start.4) | copy-done | bytes 131096
  5.1 0.0 copy-start.5
  5.1 0.8 %copy-done.5 = s32[1,16384]{1,0:T(1,128)S(1)} copy-done((s32[1,16384]{1,0:T(1,128)S(1)}, s32[1,16384]{1,0:T(1,128)}, u32[]{:S(2)}) %copy-start.5) | copy-done | bytes 65560
  5.9 0.0 copy-start.6
  5.9 0.8 %copy-done.6 = s32[1,16384]{1,0:T(1,128)S(1)} copy-done((s32[1,16384]{1,0:T(1,128)S(1)}, s32[1,16384]{1,0:T(1,128)}, u32[]{:S(2)}) %copy-start.6) | copy-done | bytes 65560
  6.8 0.0 copy-start.7
  6.8 0.8 %copy-done.7 = s32[1,16384]{1,0:T(1,128)S(1)} copy-done((s32[1,16384]{1,0:T(1,128)S(1)}, s32[1,16384]{1,0:T(1,128)}, u32[]{:S(2)}) %copy-start.7) | copy-done | bytes 65560
  7.6 61.3 %shard_map.82 = f32[2,128,512]{2,1,0:T(8,128)S(1)} custom-call(f32[2,128,512]{2,1,0:T(8,128)S(1)} %copy-done, f32[1,1024,128]{2,1,0:T(8,128)S(1)} %copy-done.1, f32[1,1024,128]{2,1,0:T(8,128)S(1)} %copy-done.2, bf16[512,128]{1,0:T(8,128)(2,1)S(1)} %bitcast.1, s32[1,16384]{1,0:T(1,128)S(1)} %copy-done.5, s32[1,16384]{1,0:T(1,128)S(1)} %copy-done.6, ...), custom_call_target="tpu_custom_call" | custom-call | tf_op jit(solution)/shard_map/pallas_call | solution.py:365
  68.9 0.8 %copy.10 = f32[2,128,512]{2,1,0:T(8,128)} copy(f32[2,128,512]{2,1,0:T(8,128)S(1)} %shard_map.82) | data formatting | bytes 1048576
Async XLA Ops:
  0.0 1.0 %copy-start = (f32[2,128,512]{2,1,0:T(8,128)S(1)}, f32[2,128,512]{2,1,0:T(8,128)}, u32[]{:S(2)}) copy-start(f32[2,128,512]{2,1,0:T(8,128)} %vol_ref.1) | copy-start | bytes 1572868
  1.0 1.0 %copy-start.1 = (f32[1,1024,128]{2,1,0:T(8,128)S(1)}, f32[1,1024,128]{2,1,0:T(8,128)}, u32[]{:S(2)}) copy-start(f32[1,1024,128]{2,1,0:T(8,128)} %meas_ref.1) | copy-start | bytes 1572868
  2.1 1.0 %copy-start.2 = (f32[1,1024,128]{2,1,0:T(8,128)S(1)}, f32[1,1024,128]{2,1,0:T(8,128)}, u32[]{:S(2)}) copy-start(f32[1,1024,128]{2,1,0:T(8,128)} %wt_ref.1) | copy-start | bytes 1572868
  3.1 1.0 %copy-start.3 = (f32[2,128,512]{2,1,0:T(8,128)S(1)}, f32[2,128,512]{2,1,0:T(8,128)}, u32[]{:S(2)}) copy-start(f32[2,128,512]{2,1,0:T(8,128)} %curv_ref.1) | copy-start | bytes 1572868
  4.2 0.9 %copy-start.4 = (bf16[8,64,128]{2,1,0:T(8,128)(2,1)S(1)}, bf16[8,64,128]{2,1,0:T(8,128)(2,1)}, u32[]{:S(2)}) copy-start(bf16[8,64,128]{2,1,0:T(8,128)(2,1)} %param.11) | copy-start | bytes 393220
  5.1 0.8 %copy-start.5 = (s32[1,16384]{1,0:T(1,128)S(1)}, s32[1,16384]{1,0:T(1,128)}, u32[]{:S(2)}) copy-start(s32[1,16384]{1,0:T(1,128)} %row_ref.1) | copy-start | bytes 196612
  5.9 0.8 %copy-start.6 = (s32[1,16384]{1,0:T(1,128)S(1)}, s32[1,16384]{1,0:T(1,128)}, u32[]{:S(2)}) copy-start(s32[1,16384]{1,0:T(1,128)} %col_ref.1) | copy-start | bytes 196612
  6.8 0.8 %copy-start.7 = (s32[1,16384]{1,0:T(1,128)S(1)}, s32[1,16384]{1,0:T(1,128)}, u32[]{:S(2)}) copy-start(s32[1,16384]{1,0:T(1,128)} %kind_ref.1) | copy-start | bytes 196612
where the time goes:
time: 70.1 us; the launch traced here: 69.7 us
  Pallas kernels  61.3 us (87%)
  local copies, waits for them, and re-layouts  8.38 us (12%)
    pallas_call x1, Pallas kernels, per_device(): pl.pallas_call(functools.partial(kernel, dims), out_shape=jax.ShapeDtypeS...  61.3 us
    unnamed x17, local copies, waits for them, and re-layouts  8.38 us

commit v1 on v0

--- a/solution.py
+++ b/solution.py
@@ -27,12 +27,13 @@
 
 def kernel(
     dims,
+    vol_hbm, meas_hbm, wt_hbm, t_hbm, row_hbm, col_hbm, kind_hbm, curv_hbm,
+    out_ref,
     vol_ref, meas_ref, wt_ref, t_ref, row_ref, col_ref, kind_ref, curv_ref,
-    out_ref,
-    vol_t, part, r_recv, l_recv, r_send, l_send, resid_t, back, sib_in, y_in,
+    vol_t, part, r_recv, l_recv, r_send, l_send, resid_t, back, back_in,
     z_send, z_lo, z_hi, y_lo, y_hi, prior,
     gs_sib, gs_y, gs_relay, g_recv, hz_s, hz_r, hy_s, hy_r,
-    rs_s, rs_r, ls_s, ls_r, bs_s, bs_r, by_s, by_r,
+    rs_s, rs_r, ls_s, ls_r, b_s, b_r, load_sem,
 ):
     vc, sc, z_local, y_own, chunk_rows, kinds, vw, windows, ypg, group = dims
     ny = y_own // chunk_rows
@@ -49,6 +50,16 @@
             device_id=where, device_id_type=MESH,
         )
 
+    loads = [
+        pltpu.make_async_copy(src, dst, load_sem.at[i])
+        for i, (src, dst) in enumerate((
+            (vol_hbm, vol_ref), (row_hbm, row_ref), (col_hbm, col_ref), (kind_hbm, kind_ref),
+            (t_hbm, t_ref), (meas_hbm, meas_ref), (wt_hbm, wt_ref), (curv_hbm, curv_ref),
+        ))
+    ]
+    for load in loads:
+        load.start()
+
     barrier = pltpu.get_barrier_semaphore()
 
     def greet(**where):
@@ -56,16 +67,14 @@
 
     for ref in (r_recv, l_recv, z_lo, z_hi, y_lo, y_hi):
         ref[...] = jnp.zeros_like(ref)
-    greet(view=sib)
-    for dy in range(1, nych):
-        greet(view=lax.rem(y + dy, nych) * 2 + c)
+    for step in range(1, vc):
+        greet(view=lax.rem(me + step, vc))
     has_left, has_right = slab > 0, slab < sc - 1
     has_low, has_high = me > 0, me < vc - 1
     pl.when(has_left)(lambda: greet(slab=slab - 1))
     pl.when(has_right)(lambda: greet(slab=slab + 1))
-    pl.when(has_low)(lambda: greet(view=me - 1))
-    pl.when(has_high)(lambda: greet(view=me + 1))
-
+
+    loads[0].wait()
     for z in range(z_local):
         for ch in range(ny):
             rows = vol_ref[z, pl.ds(ch * chunk_rows, chunk_rows), :]
@@ -79,8 +88,7 @@
 
     pl.semaphore_wait(
         barrier,
-        nych + jnp.where(has_left, 1, 0) + jnp.where(has_right, 1, 0)
-        + jnp.where(has_low, 1, 0) + jnp.where(has_high, 1, 0),
+        vc - 1 + jnp.where(has_left, 1, 0) + jnp.where(has_right, 1, 0),
     )
 
     def gather_y(dy):
@@ -101,6 +109,8 @@
     pl.when(has_low)(y_down.start)
     pl.when(has_high)(y_up.start)
 
+    for load in loads[1:5]:
+        load.wait()
     vox_count = chunk_rows * 8
     pix = meas_ref.shape[1] // windows
     vox_iota = lax.broadcasted_iota(jnp.int32, (vox_count, group), 0)
@@ -172,9 +182,11 @@
     def left_copy(i):
         return remote(l_send.at[i], l_recv.at[i], ls_s.at[i], ls_r.at[i], slab=slab - 1)
 
+    slack = 2
+
     def streams(i):
-        ri = i - slab
-        li = i - (sc - 1 - slab)
+        ri = i - slack * slab
+        li = i - slack * (sc - 1 - slab)
 
         @pl.when((ri >= 0) & (ri < windows))
         def _():
@@ -194,82 +206,72 @@
                 l_send[li] = part[order(li)] + l_recv[li]
                 left_copy(li).start()
 
-    def last_step(i, carry):
-        w = order(i)
-        value = forward(w, lax.rem(k_base + nk - 1, nk))
-        if nk > 1:
-            value = part[w] + value
-        part[w] = value
-        streams(i)
-        return carry
-
-    lax.fori_loop(0, windows, last_step, 0)
-
-    def tail_step(i, carry):
-        streams(i)
-        return carry
-
-    lax.fori_loop(windows, windows + sc - 1, tail_step, 0)
-
-    def resid_step(i, carry):
+    def residual(i):
         w = order(i)
         here = pl.ds(pl.multiple_of(w * pix, pix), pix)
         proj = part[w] + r_recv[i] + l_recv[i]
         resid = (wt_ref[0, here, :] * (meas_ref[0, here, :] - proj)).astype(bf16)
         turned = lax.dot_general(t_ref[...], resid, NT, preferred_element_type=f32)
-        resid_t[w] = jnp.concatenate(two_terms(turned), axis=1)
+        resid_t[...] = jnp.concatenate(two_terms(turned), axis=1)
+
+    def home(owner, ch):
+        at = owner * ny + ch
+        return remote(back.at[owner, ch], back_in.at[me, ch], b_s.at[at], b_r.at[me * ny + ch],
+                      view=owner)
+
+    def arrival(src, ch):
+        return remote(back.at[src, ch], back_in.at[src, ch], b_s.at[src * ny + ch],
+                      b_r.at[src * ny + ch], view=src)
+
+    def backward(w, k):
+        yc = w + windows * k
+        owner = yc // ny
+        ch = yc % ny
+        for z in range(z_local):
+            rows, spots, kind = entries(z * ypg + yc)
+            chosen = one_hot(pix_iota, rows)
+            wide = jnp.dot(
+                resid_t[...], jnp.concatenate([chosen, chosen], axis=0),
+                preferred_element_type=f32,
+            )
+            picked = wide[:vw]
+            for t in range(1, kinds):
+                picked = jnp.where(kind == t, wide[t * vw:(t + 1) * vw], picked)
+            added = lax.dot_general(
+                jnp.concatenate(two_terms(picked), axis=0), one_hot(vox_iota, spots), NT,
+                preferred_element_type=f32,
+            )
+            back[owner, ch, z] = (added[:vw] + added[vw:]).astype(bf16)
+
+        @pl.when(owner != me)
+        def _():
+            home(owner, ch).start()
+
+    def step(i, carry, go_forward, go_back):
+        if go_forward:
+            w = order(i)
+            value = forward(w, lax.rem(k_base + nk - 1, nk))
+            if nk > 1:
+                value = part[w] + value
+            part[w] = value
+        streams(i)
+        if go_back:
+            done = i - late
+            residual(done)
+            for k in range(nk):
+                backward(order(done), lax.rem(k_base + nk - 1 + k, nk))
         return carry
 
-    lax.fori_loop(0, windows, resid_step, 0)
-
-    def backward(owner):
-        def step(ch, carry):
-            yc = owner * ny + ch
-            w = lax.rem(yc, windows)
-            for z in range(z_local):
-                rows, spots, kind = entries(z * ypg + yc)
-                chosen = one_hot(pix_iota, rows)
-                wide = jnp.dot(
-                    resid_t[w], jnp.concatenate([chosen, chosen], axis=0),
-                    preferred_element_type=f32,
-                )
-                picked = wide[:vw]
-                for t in range(1, kinds):
-                    picked = jnp.where(kind == t, wide[t * vw:(t + 1) * vw], picked)
-                added = lax.dot_general(
-                    jnp.concatenate(two_terms(picked), axis=0), one_hot(vox_iota, spots), NT,
-                    preferred_element_type=f32,
-                )
-                back[owner, z * ny + ch] = (added[:vw] + added[vw:]).astype(bf16)
-            return carry
-        lax.fori_loop(0, ny, step, 0)
-
-    def to_sib(yy):
-        return remote(
-            back.at[yy * 2 + 1 - c], sib_in.at[yy], bs_s.at[yy], bs_r.at[yy], view=sib
-        )
-
-    def to_y(yy):
-        return remote(back.at[yy * 2 + c], y_in.at[y], by_s.at[yy], by_r.at[y], view=yy * 2 + c)
-
-    def from_y(yy):
-        return remote(back.at[yy * 2 + c], y_in.at[yy], by_s.at[yy], by_r.at[yy], view=yy * 2 + c)
-
-    def far(dy, carry):
-        yy = lax.rem(y + dy, nych)
-        backward(yy * 2 + 1 - c)
-        to_sib(yy).start()
-        backward(yy * 2 + c)
-        to_sib(yy).wait_recv()
-        mine = yy * 2 + c
-        back[mine] = (back[mine].astype(f32) + sib_in[yy].astype(f32)).astype(bf16)
-        to_y(yy).start()
-        return carry
-
-    lax.fori_loop(1, nych, far, 0)
-    backward(y * 2 + 1 - c)
-    to_sib(y).start()
-    backward(me)
+    late = slack * (sc - 1)
+    first, second = min(late, windows), max(late, windows)
+    run = lambda lo, hi, a, b: lax.fori_loop(
+        lo, hi, functools.partial(step, go_forward=a, go_back=b), 0
+    )
+    run(0, first, True, False)
+    loads[5].wait()
+    loads[6].wait()
+    run(first, second, late < windows, late < windows)
+    run(second, windows + late, False, True)
 
     pl.when(has_right)(z_down.wait_recv)
     pl.when(has_left)(z_up.wait_recv)
@@ -298,20 +300,20 @@
         prior[z] = pull + above - below
         below = above
 
-    to_sib(y).wait_recv()
-
-    def wait_far(dy, carry):
-        from_y(lax.rem(y + dy, nych)).wait_recv()
+    loads[7].wait()
+
+    def wait_back(i, carry):
+        src = lax.rem(me + i // ny, vc)
+        arrival(src, i % ny).wait_recv()
         return carry
 
-    lax.fori_loop(1, nych, wait_far, 0)
+    lax.fori_loop(ny, vc * ny, wait_back, 0)
 
     for z in range(z_local):
         for ch in range(ny):
-            at = z * ny + ch
-            total = back[me, at].astype(f32) + sib_in[y, at].astype(f32)
-            for dy in range(1, nych):
-                total = total + y_in[lax.rem(y + dy, nych), at].astype(f32)
+            total = back[me, ch, z].astype(f32)
+            for src in range(1, vc):
+                total = total + back_in[lax.rem(me + src, vc), ch, z].astype(f32)
             half = vox_count // 2
             tall = jnp.concatenate([total[:, :half], total[:, half:]], axis=0).T
             bp = jnp.concatenate(
@@ -331,14 +333,16 @@
     pl.when(has_high)(y_up.wait_send)
 
     def drain_y(dy, carry):
-        yy = lax.rem(y + dy, nych)
-        relay(yy * 2 + c).wait_send()
-        to_sib(yy).wait_send()
-        to_y(yy).wait_send()
+        relay(lax.rem(y + dy, nych) * 2 + c).wait_send()
         return carry
 
     lax.fori_loop(1, nych, drain_y, 0)
-    to_sib(y).wait_send()
+
+    def drain_back(i, carry):
+        home(lax.rem(me + i // ny, vc), i % ny).wait_send()
+        return carry
+
+    lax.fori_loop(ny, vc * ny, drain_back, 0)
 
     def drain_z(i, carry):
         pl.when(has_right)(lambda: right_copy(i).wait_send())
@@ -362,22 +366,24 @@
     window = (windows, 128, pix_width)
     dma = pltpu.SemaphoreType.DMA
     vmem = pl.BlockSpec(memory_space=pltpu.VMEM)
+    flat = templates.reshape(kinds * vw, pix_width)
+    args = (volume, measured, weights, flat, rows, cols, kind_ids, curvature)
+    back_tile = (vc, ny, z_local, vw, 256)
     return pl.pallas_call(
         functools.partial(kernel, dims),
         out_shape=jax.ShapeDtypeStruct(volume.shape, f32),
-        in_specs=[vmem] * 8,
+        in_specs=[pl.BlockSpec(memory_space=pl.ANY)] * 8,
         out_specs=vmem,
-        scratch_shapes=[
+        scratch_shapes=[pltpu.VMEM(arg.shape, arg.dtype) for arg in args] + [
             pltpu.VMEM((vc,) + tile, bf16),
             pltpu.VMEM(window, f32),
             pltpu.VMEM(window, f32),
             pltpu.VMEM(window, f32),
             pltpu.VMEM(window, f32),
             pltpu.VMEM(window, f32),
-            pltpu.VMEM((windows, kinds * vw, 256), bf16),
-            pltpu.VMEM((vc,) + tile, bf16),
-            pltpu.VMEM((nych,) + tile, bf16),
-            pltpu.VMEM((nych,) + tile, bf16),
+            pltpu.VMEM((kinds * vw, 256), bf16),
+            pltpu.VMEM(back_tile, bf16),
+            pltpu.VMEM(back_tile, bf16),
             pltpu.VMEM((2, y_own, x_width), bf16),
             pltpu.VMEM((y_own, x_width), bf16),
             pltpu.VMEM((y_own, x_width), bf16),
@@ -387,15 +393,12 @@
             dma, dma((nych,)), dma((nych,)), dma((vc,)),
             dma((2,)), dma((2,)), dma((2,)), dma((2,)),
             dma((windows,)), dma((windows,)), dma((windows,)), dma((windows,)),
-            dma((nych,)), dma((nych,)), dma((nych,)), dma((nych,)),
+            dma((vc * ny,)), dma((vc * ny,)), dma((8,)),
         ],
         compiler_params=pltpu.CompilerParams(
-            collective_id=0, has_side_effects=True, vmem_limit_bytes=40 * 1024 * 1024
+            collective_id=0, has_side_effects=True, vmem_limit_bytes=60 * 1024 * 1024
         ),
-    )(
-        volume, measured, weights, templates.reshape(kinds * vw, pix_width),
-        rows, cols, kind_ids, curvature,
-    )
+    )(*args)
 
 
 def solution(mesh):

time: 70.1 us -> 45.7 us (0.65)
  the two profiles are of different devices: /device:TPU:0 before, /device:TPU:1 now
where the time goes in v1:
time: 45.7 us; the launch traced here: 45.5 us
  Pallas kernels  43.6 us (95%)
  local copies, waits for them, and re-layouts  1.87 us (4%)
    pallas_call x1, Pallas kernels, per_device(): pl.pallas_call(functools.partial(kernel, dims), out_shape=jax.ShapeDtypeS...  43.6 us
    unnamed x1, local copies, waits for them, and re-layouts  1.87 us

profile of v1, /device:TPU:1, one launch (start us, length us, event | category | flops | bytes accessed | tf_op | source)
XLA Modules:
  0.0 45.5 jit_solution(16593948260097558060)
XLA Ops:
  0.0 43.6 %shard_map.82 = f32[2,128,512]{2,1,0:T(8,128)} custom-call(f32[2,128,512]{2,1,0:T(8,128)} %vol_hbm.1, f32[1,1024,128]{2,1,0:T(8,128)} %meas_hbm.1, f32[1,1024,128]{2,1,0:T(8,128)} %wt_hbm.1, bf16[512,128]{1,0:T(8,128)(2,1)} %bitcast.1, s32[1,16384]{1,0:T(1,128)} %row_hbm.1, s32[1,16384]{1,0:T(1,128)} %col_hbm.1, s32[1,16384]{1,0:T(1,128)} %kind_hbm.1, ...), custom_call_target="tpu_custom_call" | custom-call | tf_op jit(solution)/shard_map/pallas_call | solution.py:372
  43.6 1.9 %copy.10 = f32[2,128,512]{2,1,0:T(8,128)} copy(f32[2,128,512]{2,1,0:T(8,128)} %shard_map.82) | data formatting | bytes 1048576

commit v2 on v1

--- a/solution.py
+++ b/solution.py
@@ -23,6 +23,20 @@
 def two_terms(value):
     high = value.astype(bf16)
     return high, (value - high.astype(f32)).astype(bf16)
+
+
+def encode(value):
+    most = jnp.max(jnp.abs(value), axis=0, keepdims=True)
+    level = jnp.ceil(jnp.log2(jnp.maximum(most, 1e-30)) + 0.001)
+    codes = jnp.round(value * jnp.exp2(15.0 - level))
+    codes = jnp.clip(codes, -32767.0, 32767.0)
+    tail = jnp.broadcast_to(level, (16, value.shape[1]))
+    return jnp.concatenate([codes, tail], axis=0).astype(jnp.int32).astype(jnp.int16)
+
+
+def decode(message):
+    wide = message.astype(jnp.int32).astype(f32)
+    return wide[:-16] * jnp.exp2(wide[-16:-15] - 15.0)
 
 
 def kernel(
@@ -113,8 +127,8 @@
         load.wait()
     vox_count = chunk_rows * 8
     pix = meas_ref.shape[1] // windows
-    vox_iota = lax.broadcasted_iota(jnp.int32, (vox_count, group), 0)
-    pix_iota = lax.broadcasted_iota(jnp.int32, (pix, group), 0)
+    vox_iota = lax.broadcasted_iota(jnp.int16, (vox_count, group), 0)
+    pix_iota = lax.broadcasted_iota(jnp.int16, (pix, group), 0)
 
     def entries(q):
         here = pl.ds(pl.multiple_of(q * group, group), group)
@@ -123,7 +137,7 @@
         return row_ref[:, here] & (pix - 1), spot, kind_ref[:, here]
 
     def one_hot(iota, spot):
-        return jnp.where(iota == spot, 1.0, 0.0).astype(bf16)
+        return jnp.where(iota == spot.astype(jnp.int16), jnp.ones((), bf16), jnp.zeros((), bf16))
 
     def relay(o):
         return remote(vol_t.at[o], vol_t.at[o], gs_relay.at[o // 2], g_recv.at[o], view=sib)
@@ -146,9 +160,11 @@
             rows, spots, kind = entries(z * ypg + yc)
             picked = jnp.dot(
                 vol_t[owner, z * ny + ch], one_hot(vox_iota, spots), preferred_element_type=f32
-            )
+            ).astype(bf16)
+            kind = jnp.broadcast_to(kind.astype(jnp.int16), picked.shape)
+            none = jnp.zeros_like(picked)
             spread = jnp.concatenate(
-                [jnp.where(kind == t, picked, 0.0).astype(bf16) for t in range(kinds)], axis=0
+                [jnp.where(kind == t, picked, none) for t in range(kinds)], axis=0
             )
             added = lax.dot_general(
                 one_hot(pix_iota, rows), spread, NT, preferred_element_type=f32
@@ -194,7 +210,7 @@
 
             @pl.when(has_right)
             def _():
-                r_send[ri] = part[order(ri)] + r_recv[ri]
+                r_send[ri] = encode(part[order(ri)] + decode(r_recv[ri]))
                 right_copy(ri).start()
 
         @pl.when((li >= 0) & (li < windows))
@@ -203,13 +219,13 @@
 
             @pl.when(has_left)
             def _():
-                l_send[li] = part[order(li)] + l_recv[li]
+                l_send[li] = encode(part[order(li)] + decode(l_recv[li]))
                 left_copy(li).start()
 
     def residual(i):
         w = order(i)
         here = pl.ds(pl.multiple_of(w * pix, pix), pix)
-        proj = part[w] + r_recv[i] + l_recv[i]
+        proj = part[w] + decode(r_recv[i]) + decode(l_recv[i])
         resid = (wt_ref[0, here, :] * (meas_ref[0, here, :] - proj)).astype(bf16)
         turned = lax.dot_general(t_ref[...], resid, NT, preferred_element_type=f32)
         resid_t[...] = jnp.concatenate(two_terms(turned), axis=1)
@@ -364,6 +380,7 @@
     tile = (z_local * ny, vw, 256)
     dims = (vc, sc, z_local, y_own, chunk_rows, kinds, vw, windows, ypg, group)
     window = (windows, 128, pix_width)
+    message = (windows, 128 + 16, pix_width)
     dma = pltpu.SemaphoreType.DMA
     vmem = pl.BlockSpec(memory_space=pltpu.VMEM)
     flat = templates.reshape(kinds * vw, pix_width)
@@ -377,10 +394,10 @@
         scratch_shapes=[pltpu.VMEM(arg.shape, arg.dtype) for arg in args] + [
             pltpu.VMEM((vc,) + tile, bf16),
             pltpu.VMEM(window, f32),
-            pltpu.VMEM(window, f32),
-            pltpu.VMEM(window, f32),
-            pltpu.VMEM(window, f32),
-            pltpu.VMEM(window, f32),
+            pltpu.VMEM(message, jnp.int16),
+            pltpu.VMEM(message, jnp.int16),
+            pltpu.VMEM(message, jnp.int16),
+            pltpu.VMEM(message, jnp.int16),
             pltpu.VMEM((kinds * vw, 256), bf16),
             pltpu.VMEM(back_tile, bf16),
             pltpu.VMEM(back_tile, bf16),

time: 45.7 us -> 43.5 us (0.952)
  Pallas kernels: 43.6 us -> 41.5 us
    pallas_call x1, Pallas kernels: 43.6 us -> 41.5 us  [per_device(): pl.pallas_call(functools.partial(kernel, dims), out_shape=jax.ShapeDtypeS...]
where the time goes in v2:
time: 43.5 us; the launch traced here: 43.4 us
  Pallas kernels  41.5 us (95%)
  local copies, waits for them, and re-layouts  1.87 us (4%)
    pallas_call x1, Pallas kernels, per_device(): pl.pallas_call(functools.partial(kernel, dims), out_shape=jax.ShapeDtypeS...  41.5 us
    unnamed x1, local copies, waits for them, and re-layouts  1.87 us

profile of v2, /device:TPU:1, one launch (start us, length us, event | category | flops | bytes accessed | tf_op | source)
XLA Modules:
  0.0 43.4 jit_solution(17774941132648719050)
XLA Ops:
  0.0 41.5 %shard_map.82 = f32[2,128,512]{2,1,0:T(8,128)} custom-call(f32[2,128,512]{2,1,0:T(8,128)} %vol_hbm.1, f32[1,1024,128]{2,1,0:T(8,128)} %meas_hbm.1, f32[1,1024,128]{2,1,0:T(8,128)} %wt_hbm.1, bf16[512,128]{1,0:T(8,128)(2,1)} %bitcast.1, s32[1,16384]{1,0:T(1,128)} %row_hbm.1, s32[1,16384]{1,0:T(1,128)} %col_hbm.1, s32[1,16384]{1,0:T(1,128)} %kind_hbm.1, ...), custom_call_target="tpu_custom_call" | custom-call | tf_op jit(solution)/shard_map/pallas_call | solution.py:389
  41.5 1.9 %copy.10 = f32[2,128,512]{2,1,0:T(8,128)} copy(f32[2,128,512]{2,1,0:T(8,128)} %shard_map.82) | data formatting | bytes 1048576

commit v3 on v2

--- a/solution.py
+++ b/solution.py
@@ -198,7 +198,7 @@
     def left_copy(i):
         return remote(l_send.at[i], l_recv.at[i], ls_s.at[i], ls_r.at[i], slab=slab - 1)
 
-    slack = 2
+    slack = 3
 
     def streams(i):
         ri = i - slack * slab
@@ -318,15 +318,10 @@
 
     loads[7].wait()
 
-    def wait_back(i, carry):
-        src = lax.rem(me + i // ny, vc)
-        arrival(src, i % ny).wait_recv()
-        return carry
-
-    lax.fori_loop(ny, vc * ny, wait_back, 0)
-
-    for z in range(z_local):
-        for ch in range(ny):
+    for ch in range(ny):
+        for src in range(1, vc):
+            arrival(lax.rem(me + src, vc), ch).wait_recv()
+        for z in range(z_local):
             total = back[me, ch, z].astype(f32)
             for src in range(1, vc):
                 total = total + back_in[lax.rem(me + src, vc), ch, z].astype(f32)

time: 43.5 us -> 42.5 us (0.977)
  Pallas kernels: 41.5 us -> 40.4 us
    pallas_call x1, Pallas kernels: 41.5 us -> 40.4 us  [per_device(): pl.pallas_call(functools.partial(kernel, dims), out_shape=jax.ShapeDtypeS...]
where the time goes in v3:
time: 42.5 us; the launch traced here: 42.3 us
  Pallas kernels  40.4 us (95%)
  local copies, waits for them, and re-layouts  1.87 us (4%)
    pallas_call x1, Pallas kernels, per_device(): pl.pallas_call(functools.partial(kernel, dims), out_shape=jax.ShapeDtypeS...  40.4 us
    unnamed x1, local copies, waits for them, and re-layouts  1.87 us

profile of v3, /device:TPU:1, one launch (start us, length us, event | category | flops | bytes accessed | tf_op | source)
XLA Modules:
  0.0 42.3 jit_solution(3506292149614170648)
XLA Ops:
  0.0 40.4 %shard_map.82 = f32[2,128,512]{2,1,0:T(8,128)} custom-call(f32[2,128,512]{2,1,0:T(8,128)} %vol_hbm.1, f32[1,1024,128]{2,1,0:T(8,128)} %meas_hbm.1, f32[1,1024,128]{2,1,0:T(8,128)} %wt_hbm.1, bf16[512,128]{1,0:T(8,128)(2,1)} %bitcast.1, s32[1,16384]{1,0:T(1,128)} %row_hbm.1, s32[1,16384]{1,0:T(1,128)} %col_hbm.1, s32[1,16384]{1,0:T(1,128)} %kind_hbm.1, ...), custom_call_target="tpu_custom_call" | custom-call | tf_op jit(solution)/shard_map/pallas_call | solution.py:384
  40.4 1.9 %copy.10 = f32[2,128,512]{2,1,0:T(8,128)} copy(f32[2,128,512]{2,1,0:T(8,128)} %shard_map.82) | data formatting | bytes 1048576
